TPU v7x, 32 devices: a whole 2x2x4 slice. The times are simulated.
32 devices in a mesh: gx: 2 (over core), gy: 4 (over y, x), gz: 4 (over z).
Axes of the slice: x: 2, y: 2, z: 4, core: 2. Of those that a mesh axis runs over, the one named last changes fastest.
Arguments:
- dual_matrix: float32 [2, 4, 4, 1536, 1536], P('gx', 'gy', 'gz'), may hold values from -1 to 4, as said below
- modes: float32 [2, 4, 4, 6, 1536], P('gx', 'gy', 'gz'), may hold values from -0.15625 to 0.15625
- coarse_rows: float32 [192, 192], P(('gx', 'gy', 'gz')), may hold values from -0.2 to 0.4, as said below
- loads: float32 [2, 4, 4, 8, 6, 128], P('gx', 'gy', 'gz'), may hold values from -40 to 40
- face_counts: int32 [2, 4, 4, 3], replicated, may hold values from 32 to 128
- contact: int32 [2, 4, 4, 6, 128], P('gx', 'gy', 'gz'), may hold values 0 or 1
Outputs:
- multipliers: float32 [2, 4, 4, 8, 6, 128], P('gx', 'gy', 'gz')
- residual: float32 [2, 4, 4, 8, 6, 128], P('gx', 'gy', 'gz')
Inputs may be any that keep to these rules, and one draw needn't show every extreme that they name: `dual_matrix`: every subdomain's matrix is symmetric positive definite. `coarse_rows`: the coarse operator is symmetric positive definite.
All inputs are finite; a program needn't handle non-finite values. No bound on the sum of `contact` on one device may be relied on, other than what follows from the above.
Results may differ from a plain program's by a relative error of at most 0.0003.
Values sent between devices are 32-bit elements; how exact they have to be, the bound alone decides.
A program may use at most 128 MiB of HBM per device.

v0:
```python
import jax
import jax.numpy as jnp
from jax import lax
from jax.sharding import PartitionSpec as P

ITERS = 4


highest = lax.Precision.HIGHEST


def from_behind(block, axis, distance):
    devices = range(lax.axis_size(axis))
    route = [((i - distance) % len(devices), i) for i in devices]
    return lax.ppermute(block, axis, route)


def trade(upper_faces, lower_faces):
    from_below = [
        from_behind(upper_faces[0], "gx", 1),
        from_behind(upper_faces[1], "gy", 1),
        from_behind(upper_faces[2], "gz", 1),
    ]
    from_above = [
        from_behind(lower_faces[0], "gx", -1),
        from_behind(lower_faces[1], "gy", -1),
        from_behind(lower_faces[2], "gz", -1),
    ]
    return (from_below, from_above)


def spread_faces(owned_vec):
    upper_faces = [owned_vec[..., 2 * grid_axis + 1, :] for grid_axis in range(3)]
    lower_faces = [owned_vec[..., 2 * grid_axis, :] for grid_axis in range(3)]
    from_below, from_above = trade(upper_faces, lower_faces)
    faces = []
    for grid_axis in range(3):
        faces.append(jnp.concatenate([from_below[grid_axis], lower_faces[grid_axis]], axis=-1))
        faces.append(jnp.concatenate([upper_faces[grid_axis], from_above[grid_axis]], axis=-1))
    return jnp.stack(faces, axis=-2)


def collect_faces(local_form):
    half_width = local_form.shape[-1] // 2
    upper_faces = [local_form[..., 2 * grid_axis + 1, half_width:] for grid_axis in range(3)]
    lower_faces = [local_form[..., 2 * grid_axis, :half_width] for grid_axis in range(3)]
    from_below, from_above = trade(upper_faces, lower_faces)
    pieces = []
    for grid_axis in range(3):
        pieces.append(local_form[..., 2 * grid_axis, half_width:] + from_below[grid_axis])
        pieces.append(local_form[..., 2 * grid_axis + 1, :half_width] + from_above[grid_axis])
    return jnp.stack(pieces, axis=-2)


def coarse_weights(flattened, own_modes, coarse_rows):
    on_modes = jnp.einsum("jm,km->jk", own_modes, flattened, precision=highest)
    return jnp.dot(
        coarse_rows,
        lax.all_gather(on_modes, ("gx", "gy", "gz"), axis=0, tiled=True),
        precision=highest,
    )


def on_device(dual_matrix, modes, coarse_rows, loads, face_counts, contact):
    half_width = loads.shape[-1]
    case_count = loads.shape[3]
    grid_pos = [lax.axis_index("gx"), lax.axis_index("gy"), lax.axis_index("gz")]
    grid_sizes = [lax.axis_size("gx"), lax.axis_size("gy"), lax.axis_size("gz")]

    def counts_at(where):
        return lax.dynamic_slice(
            face_counts, (where[0], where[1], where[2], 0), (1, 1, 1, 3)
        ).reshape(3)

    own_counts = counts_at(grid_pos)
    positions = jnp.arange(half_width, dtype=jnp.int32)
    own_masks = []
    local_masks = []
    for grid_axis in range(3):
        lower_pos = list(grid_pos)
        lower_pos[grid_axis] = (grid_pos[grid_axis] - 1 + grid_sizes[grid_axis]) % grid_sizes[
            grid_axis
        ]
        lower_count = counts_at(lower_pos)[grid_axis]
        lower_row = (positions < lower_count).astype(jnp.float32)
        upper_row = (positions < own_counts[grid_axis]).astype(jnp.float32)
        own_masks.extend([lower_row, upper_row])
        local_masks.extend(
            [jnp.concatenate([lower_row, lower_row]), jnp.concatenate([upper_row, upper_row])]
        )
    active_own = jnp.stack(own_masks).reshape(1, 1, 1, 1, 6, half_width)
    is_contact = contact[:, :, :, None] == 1
    matrix = dual_matrix[0, 0, 0]
    own_modes = modes[0, 0, 0]

    def local_coarse(local_form):
        flattened = local_form.reshape(case_count, -1)
        weights = coarse_weights(flattened, own_modes, coarse_rows)
        return jnp.einsum("jk,jm->km", weights, own_modes, precision=highest).reshape(
            local_form.shape
        )

    def project(vector):
        return vector - collect_faces(local_coarse(spread_faces(vector))) * active_own

    start_vector = loads * active_own

    def partial_inner(first, second):
        return jnp.sum(first * second, axis=(0, 1, 2, 4, 5))

    multipliers = jnp.zeros(loads.shape, jnp.float32)
    residual = start_vector

    def energy_sum(first, second):
        return lax.psum(partial_inner(first, second), ("gx", "gy", "gz")).reshape(-1, 1, 1)

    precond = project(residual)
    direction = precond
    energy = energy_sum(residual, precond)
    for rounds in range(ITERS):
        local_local_form = spread_faces(direction)
        local_flattened = local_local_form.reshape(case_count, -1)
        dual_image = (
            collect_faces(
                jnp.dot(local_flattened, matrix, precision=highest).reshape(local_local_form.shape)
            )
            * active_own
        )
        curvature = lax.psum(partial_inner(direction, dual_image), ("gx", "gy", "gz")).reshape(
            -1, 1, 1
        )
        step_size = energy / curvature
        updated = multipliers + step_size * direction
        multipliers = jnp.where(is_contact, jnp.maximum(updated, 0.0), updated)
        residual = residual - step_size * dual_image
        if rounds + 1 < ITERS:
            precond = project(residual)
            energy_next = energy_sum(residual, precond)
            direction = precond + energy_next / energy * direction
            energy = energy_next
    return (multipliers, residual)


def solution(mesh):
    return jax.shard_map(
        on_device,
        mesh=mesh,
        in_specs=(
            P("gx", "gy", "gz", None, None),
            P("gx", "gy", "gz", None, None),
            P(("gx", "gy", "gz"), None),
            P("gx", "gy", "gz", None, None, None),
            P(),
            P("gx", "gy", "gz", None, None),
        ),
        out_specs=(P("gx", "gy", "gz", None, None, None), P("gx", "gy", "gz", None, None, None)),
        check_vma=False,
    )
```

profile of v0, /device:TPU:0, one launch (start us, length us, event | category | flops | bytes accessed | tf_op | source)
XLA Modules:
  0.0 787.7 jit_solution(9719686072488246595)
XLA Ops:
  7.4 2.9 collective-permute-start.2
  11.3 2.1 collective-permute-start.4
  14.1 2.1 collective-permute-start.5
  18.8 67.1 %all-gather = f32[32,6,8]{2,1,0:T(8,128)S(1)} all-gather(f32[1,6,8]{2,1,0:T(8,128)S(1)} %bitcast.1086), channel_id=1, replica_groups=mesh['gx'=2,'gy'=4,'gz'=4] {'gx','gy','gz'}, dimensions={0}, use_global_device_ids=true | all-gather | bytes 6336 | tf_op jit(solution)/shard_map/all_gather | solution.py:59
  86.5 2.4 collective-permute-start.6
  89.0 1.6 collective-permute-start.8
  91.9 3.9 collective-permute-start.11
  95.8 4.1 collective-permute-done.9
  100.8 9.6 %copy.36 = f32[1,1,1,1536,1536]{3,4,2,1,0:T(8,128)} copy(f32[1,1,1,1536,1536]{4,3,2,1,0:T(8,128)} %param.6) | data formatting | bytes 18874368 | tf_op args[0]
  110.9 3.8 collective-permute-start.14
  114.7 3.9 collective-permute-start.17
  120.1 10.1 %convolution_bitcast_fusion.6 = f32[1,1,1,8,6,256]{5,3,4,2,1,0:T(8,128)S(1)} fusion(f32[8,1536,1]{1,0,2:T(8,128)S(1)} %bitcast.1078, f32[6,256,1536]{2,1,0:T(8,128)} %bitcast.1070), kind=kOutput, calls=%fused_computation.6 | convolution fusion | flops 226492416 | bytes 9535488 | tf_op jit(solution)/shard_map/dot_general | solution.py:125
  130.8 2.9 collective-permute-start.20
  134.9 2.8 collective-permute-start.23
  139.4 41.9 %all-reduce = (f32[8]{0:T(128)S(1)}, f32[8]{0:T(128)S(1)}) all-reduce(f32[8]{0:T(128)S(1)} %get-tuple-element.3, f32[8]{0:T(128)S(1)} %get-tuple-element.2), channel_id=1, replica_groups=mesh['gx'=2,'gy'=4,'gz'=4] {'gx','gy','gz'}, use_global_device_ids=true, to_apply=%region_1.2 | all-reduce | flops 16 | bytes 128 | tf_op jit(solution)/shard_map/psum | solution.py:115
  181.9 2.3 collective-permute-start.26
  185.5 1.8 collective-permute-start.28
  187.4 2.0 collective-permute-start.29
  189.4 1.5 collective-permute-done.28
  191.2 67.3 %all-gather.1 = f32[32,6,8]{2,1,0:T(8,128)S(1)} all-gather(f32[1,6,8]{2,1,0:T(8,128)S(1)} %bitcast.1087), channel_id=1, replica_groups=mesh['gx'=2,'gy'=4,'gz'=4] {'gx','gy','gz'}, dimensions={0}, use_global_device_ids=true | all-gather | bytes 6336 | tf_op jit(solution)/shard_map/all_gather | solution.py:59
  259.1 2.5 collective-permute-start.30
  262.7 1.9 collective-permute-start.33
  264.6 3.8 collective-permute-start.35
  268.4 3.6 collective-permute-done.33
  272.2 42.4 %psum.58 = f32[8]{0:T(128)S(1)} all-reduce(f32[8]{0:T(128)S(1)} %multiply_reduce_fusion.5), channel_id=1, replica_groups=mesh['gx'=2,'gy'=4,'gz'=4] {'gx','gy','gz'}, use_global_device_ids=true, to_apply=%region_5.6 | all-reduce | flops 8 | bytes 64 | tf_op jit(solution)/shard_map/psum | solution.py:115
  315.2 2.3 collective-permute-start.38
  318.9 2.1 collective-permute-start.40
  321.1 1.7 collective-permute-start.41
  324.7 10.1 %convolution_bitcast_fusion.4 = f32[1,1,1,8,6,256]{5,3,4,2,1,0:T(8,128)S(1)} fusion(f32[8,1536,1]{1,0,2:T(8,128)S(1)} %bitcast.1079, f32[6,256,1536]{2,1,0:T(8,128)} %bitcast.1071), kind=kOutput, calls=%fused_computation.4 | convolution fusion | flops 226492416 | bytes 9535488 | tf_op jit(solution)/shard_map/dot_general | solution.py:125
  336.1 2.2 collective-permute-start.45
  339.7 2.4 collective-permute-start.47
  342.2 1.5 collective-permute-done.46
  343.8 39.2 %psum.59 = f32[8]{0:T(128)S(1)} all-reduce(f32[8]{0:T(128)S(1)} %multiply_reduce_fusion.4), channel_id=1, replica_groups=mesh['gx'=2,'gy'=4,'gz'=4] {'gx','gy','gz'}, use_global_device_ids=true, to_apply=%region_7.8 | all-reduce | flops 8 | bytes 64 | tf_op jit(solution)/shard_map/psum | solution.py:129
  383.7 2.3 collective-permute-start.50
  386.9 2.2 collective-permute-start.52
  389.1 1.6 collective-permute-start.53
  393.0 66.9 %all-gather.2 = f32[32,6,8]{2,1,0:T(8,128)S(1)} all-gather(f32[1,6,8]{2,1,0:T(8,128)S(1)} %bitcast.1088), channel_id=1, replica_groups=mesh['gx'=2,'gy'=4,'gz'=4] {'gx','gy','gz'}, dimensions={0}, use_global_device_ids=true | all-gather | bytes 6336 | tf_op jit(solution)/shard_map/all_gather | solution.py:59
  460.4 2.5 collective-permute-start.54
  466.0 3.8 collective-permute-start.59
  469.8 4.1 collective-permute-done.57
  474.1 42.4 %psum.60 = f32[8]{0:T(128)S(1)} all-reduce(f32[8]{0:T(128)S(1)} %multiply_reduce_fusion.3), channel_id=1, replica_groups=mesh['gx'=2,'gy'=4,'gz'=4] {'gx','gy','gz'}, use_global_device_ids=true, to_apply=%region_9.10 | all-reduce | flops 8 | bytes 64 | tf_op jit(solution)/shard_map/psum | solution.py:115
  517.1 2.3 collective-permute-start.62
  520.8 2.1 collective-permute-start.64
  523.0 1.7 collective-permute-start.65
  526.6 10.1 %convolution_bitcast_fusion.2 = f32[1,1,1,8,6,256]{5,3,4,2,1,0:T(8,128)S(1)} fusion(f32[8,1536,1]{1,0,2:T(8,128)S(1)} %bitcast.1080, f32[6,256,1536]{2,1,0:T(8,128)} %bitcast.1072), kind=kOutput, calls=%fused_computation.2 | convolution fusion | flops 226492416 | bytes 9535488 | tf_op jit(solution)/shard_map/dot_general | solution.py:125
  537.9 2.2 collective-permute-start.69
  541.6 2.4 collective-permute-start.71
  544.1 1.5 collective-permute-done.70
  545.7 39.2 %psum.61 = f32[8]{0:T(128)S(1)} all-reduce(f32[8]{0:T(128)S(1)} %multiply_reduce_fusion.2), channel_id=1, replica_groups=mesh['gx'=2,'gy'=4,'gz'=4] {'gx','gy','gz'}, use_global_device_ids=true, to_apply=%region_11.12 | all-reduce | flops 8 | bytes 64 | tf_op jit(solution)/shard_map/psum | solution.py:129
  585.6 2.3 collective-permute-start.74
  588.8 2.2 collective-permute-start.76
  591.0 1.6 collective-permute-start.77
  594.9 66.9 %all-gather.3 = f32[32,6,8]{2,1,0:T(8,128)S(1)} all-gather(f32[1,6,8]{2,1,0:T(8,128)S(1)} %bitcast.1089), channel_id=1, replica_groups=mesh['gx'=2,'gy'=4,'gz'=4] {'gx','gy','gz'}, dimensions={0}, use_global_device_ids=true | all-gather | bytes 6336 | tf_op jit(solution)/shard_map/all_gather | solution.py:59
  662.3 2.5 collective-permute-start.78
  667.9 3.8 collective-permute-start.83
  671.7 4.1 collective-permute-done.81
  676.0 42.4 %psum.62 = f32[8]{0:T(128)S(1)} all-reduce(f32[8]{0:T(128)S(1)} %multiply_reduce_fusion.1), channel_id=1, replica_groups=mesh['gx'=2,'gy'=4,'gz'=4] {'gx','gy','gz'}, use_global_device_ids=true, to_apply=%region_13.14 | all-reduce | flops 8 | bytes 64 | tf_op jit(solution)/shard_map/psum | solution.py:115
  719.0 2.3 collective-permute-start.86
  722.7 2.1 collective-permute-start.88
  724.8 1.7 collective-permute-start.89
  728.5 10.1 %convolution_bitcast_fusion = f32[1,1,1,8,6,256]{5,3,4,2,1,0:T(8,128)S(1)} fusion(f32[8,1536,1]{1,0,2:T(8,128)S(1)} %bitcast.1081, f32[6,256,1536]{2,1,0:T(8,128)} %bitcast.1073), kind=kOutput, calls=%fused_computation | convolution fusion | flops 226492416 | bytes 9535488 | tf_op jit(solution)/shard_map/dot_general | solution.py:125
  739.9 2.2 collective-permute-start.93
  743.5 2.4 collective-permute-start.95
  747.7 39.3 %psum.63 = f32[8]{0:T(128)S(1)} all-reduce(f32[8]{0:T(128)S(1)} %multiply_reduce_fusion), channel_id=1, replica_groups=mesh['gx'=2,'gy'=4,'gz'=4] {'gx','gy','gz'}, use_global_device_ids=true, to_apply=%region_15.16 | all-reduce | flops 8 | bytes 64 | tf_op jit(solution)/shard_map/psum | solution.py:129
  (316 shorter events, 60.6 us)
Async XLA Ops:
  6.9 7.2 collective-permute-start
  7.3 8.9 %collective-permute-start.1 = (f32[1,1,1,8,128]{4,3,2,1,0:T(8,128)S(1)}, f32[1,1,1,8,128]{4,3,2,1,0:T(8,128)S(1)}, u32[]{:S(2)}, u32[]{:S(2)}) collective-permute-start(f32[1,1,1,8,128]{4,3,2,1,0:T(8,128)S(1)} %get-tuple-element.100), channel_id=1, source_target_pairs={{16,0},{0,16},{17,1},{1,17},{18,2},{2,18},{19,3},{3,19},{20,4},{4,... | collective-permute-start | bytes 12296 | tf_op jit(solution)/shard_map/ppermute | solution.py:15
  7.4 8.8 %collective-permute-start.2 = (f32[1,1,1,8,128]{4,3,2,1,0:T(8,128)S(1)}, f32[1,1,1,8,128]{4,3,2,1,0:T(8,128)S(1)}, u32[]{:S(2)}, u32[]{:S(2)}) collective-permute-start(f32[1,1,1,8,128]{4,3,2,1,0:T(8,128)S(1)} %get-tuple-element.99), channel_id=1, source_target_pairs={{12,0},{0,4},{4,8},{8,12},{13,1},{1,5},{5,9},{9,13},{14,2},{2,6},{... | collective-permute-start | bytes 12296 | tf_op jit(solution)/shard_map/ppermute | solution.py:15
  10.3 5.9 collective-permute-start.3
  11.3 5.7 collective-permute-start.4
  86.5 5.4 collective-permute-start.6
  88.9 6.9 collective-permute-start.7
  89.0 6.8 collective-permute-start.8
  90.6 9.4 %collective-permute-start.9 = (f32[1,1,1,8,128]{4,3,2,1,0:T(8,128)S(1)}, f32[1,1,1,8,128]{4,3,2,1,0:T(8,128)S(1)}, u32[]{:S(2)}, u32[]{:S(2)}) collective-permute-start(f32[1,1,1,8,128]{4,3,2,1,0:T(8,128)S(1)} %get-tuple-element.50), channel_id=1, source_target_pairs={{4,0},{8,4},{12,8},{0,12},{5,1},{9,5},{13,9},{1,13},{6,2},{10,6},{... | collective-permute-start | bytes 12296 | tf_op jit(solution)/shard_map/ppermute | solution.py:15
  91.9 8.0 %collective-permute-start.10 = (f32[1,1,1,8,128]{4,3,2,1,0:T(8,128)S(1)}, f32[1,1,1,8,128]{4,3,2,1,0:T(8,128)S(1)}, u32[]{:S(2)}, u32[]{:S(2)}) collective-permute-start(f32[1,1,1,8,128]{4,3,2,1,0:T(8,128)S(1)} %get-tuple-element.49), channel_id=1, source_target_pairs={{3,0},{0,1},{1,2},{2,3},{7,4},{4,5},{5,6},{6,7},{11,8},{8,9},{9,10... | collective-permute-start | bytes 12296 | tf_op jit(solution)/shard_map/ppermute | solution.py:15
  91.9 8.0 %collective-permute-start.11 = (f32[1,1,1,8,128]{4,3,2,1,0:T(8,128)S(1)}, f32[1,1,1,8,128]{4,3,2,1,0:T(8,128)S(1)}, u32[]{:S(2)}, u32[]{:S(2)}) collective-permute-start(f32[1,1,1,8,128]{4,3,2,1,0:T(8,128)S(1)} %get-tuple-element.48), channel_id=1, source_target_pairs={{1,0},{2,1},{3,2},{0,3},{5,4},{6,5},{7,6},{4,7},{9,8},{10,9},{11,1... | collective-permute-start | bytes 12296 | tf_op jit(solution)/shard_map/ppermute | solution.py:15
  100.7 14.0 %collective-permute-start.12 = (f32[1,1,1,8,128]{4,3,2,1,0:T(8,128)S(1)}, f32[1,1,1,8,128]{4,3,2,1,0:T(8,128)S(1)}, u32[]{:S(2)}, u32[]{:S(2)}) collective-permute-start(f32[1,1,1,8,128]{4,3,2,1,0:T(8,128)S(1)} %get-tuple-element.95), channel_id=1, source_target_pairs={{16,0},{0,16},{17,1},{1,17},{18,2},{2,18},{19,3},{3,19},{20,4},{4,... | collective-permute-start | bytes 12296 | tf_op jit(solution)/shard_map/ppermute | solution.py:15
  110.5 8.1 %collective-permute-start.13 = (f32[1,1,1,8,128]{4,3,2,1,0:T(8,128)S(1)}, f32[1,1,1,8,128]{4,3,2,1,0:T(8,128)S(1)}, u32[]{:S(2)}, u32[]{:S(2)}) collective-permute-start(f32[1,1,1,8,128]{4,3,2,1,0:T(8,128)S(1)} %get-tuple-element.94), channel_id=1, source_target_pairs={{16,0},{0,16},{17,1},{1,17},{18,2},{2,18},{19,3},{3,19},{20,4},{4,... | collective-permute-start | bytes 12296 | tf_op jit(solution)/shard_map/ppermute | solution.py:15
  110.9 7.7 collective-permute-start.14
  130.3 7.4 collective-permute-start.19
  130.8 6.9 collective-permute-start.20
  133.7 5.4 collective-permute-start.22
  181.3 6.0 collective-permute-start.24
  181.4 8.0 %collective-permute-start.25 = (f32[1,1,1,8,128]{4,3,2,1,0:T(8,128)S(1)}, f32[1,1,1,8,128]{4,3,2,1,0:T(8,128)S(1)}, u32[]{:S(2)}, u32[]{:S(2)}) collective-permute-start(f32[1,1,1,8,128]{4,3,2,1,0:T(8,128)S(1)} %get-tuple-element.88), channel_id=1, source_target_pairs={{16,0},{0,16},{17,1},{1,17},{18,2},{2,18},{19,3},{3,19},{20,4},{4,... | collective-permute-start | bytes 12296 | tf_op jit(solution)/shard_map/ppermute | solution.py:15
  181.9 7.5 collective-permute-start.26
  259.1 5.5 collective-permute-start.30
  261.6 6.8 collective-permute-start.31
  261.7 6.8 collective-permute-start.32
  262.7 9.4 %collective-permute-start.33 = (f32[1,1,1,8,128]{4,3,2,1,0:T(8,128)S(1)}, f32[1,1,1,8,128]{4,3,2,1,0:T(8,128)S(1)}, u32[]{:S(2)}, u32[]{:S(2)}) collective-permute-start(f32[1,1,1,8,128]{4,3,2,1,0:T(8,128)S(1)} %get-tuple-element.38), channel_id=1, source_target_pairs={{4,0},{8,4},{12,8},{0,12},{5,1},{9,5},{13,9},{1,13},{6,2},{10,6},{... | collective-permute-start | bytes 12296 | tf_op jit(solution)/shard_map/ppermute | solution.py:15
  264.6 7.5 collective-permute-start.34
  264.6 7.5 collective-permute-start.35
  314.7 6.4 collective-permute-start.36
  314.7 8.1 %collective-permute-start.37 = (f32[1,1,1,8,128]{4,3,2,1,0:T(8,128)S(1)}, f32[1,1,1,8,128]{4,3,2,1,0:T(8,128)S(1)}, u32[]{:S(2)}, u32[]{:S(2)}) collective-permute-start(f32[1,1,1,8,128]{4,3,2,1,0:T(8,128)S(1)} %get-tuple-element.82), channel_id=1, source_target_pairs={{16,0},{0,16},{17,1},{1,17},{18,2},{2,18},{19,3},{3,19},{20,4},{4,... | collective-permute-start | bytes 12296 | tf_op jit(solution)/shard_map/ppermute | solution.py:15
  315.2 7.6 collective-permute-start.38
  334.9 7.3 collective-permute-start.43
  335.4 6.8 collective-permute-start.44
  336.1 6.1 collective-permute-start.45
  338.3 5.4 collective-permute-start.46
  383.2 6.0 collective-permute-start.48
  383.2 7.5 collective-permute-start.49
  383.7 7.1 collective-permute-start.50
  460.4 5.5 collective-permute-start.54
  463.0 6.8 collective-permute-start.55
  463.0 6.8 collective-permute-start.56
  464.5 9.4 %collective-permute-start.57 = (f32[1,1,1,8,128]{4,3,2,1,0:T(8,128)S(1)}, f32[1,1,1,8,128]{4,3,2,1,0:T(8,128)S(1)}, u32[]{:S(2)}, u32[]{:S(2)}) collective-permute-start(f32[1,1,1,8,128]{4,3,2,1,0:T(8,128)S(1)} %get-tuple-element.26), channel_id=1, source_target_pairs={{4,0},{8,4},{12,8},{0,12},{5,1},{9,5},{13,9},{1,13},{6,2},{10,6},{... | collective-permute-start | bytes 12296 | tf_op jit(solution)/shard_map/ppermute | solution.py:15
  466.0 8.0 %collective-permute-start.58 = (f32[1,1,1,8,128]{4,3,2,1,0:T(8,128)S(1)}, f32[1,1,1,8,128]{4,3,2,1,0:T(8,128)S(1)}, u32[]{:S(2)}, u32[]{:S(2)}) collective-permute-start(f32[1,1,1,8,128]{4,3,2,1,0:T(8,128)S(1)} %get-tuple-element.25), channel_id=1, source_target_pairs={{3,0},{0,1},{1,2},{2,3},{7,4},{4,5},{5,6},{6,7},{11,8},{8,9},{9,10... | collective-permute-start | bytes 12296 | tf_op jit(solution)/shard_map/ppermute | solution.py:15
  466.0 8.0 %collective-permute-start.59 = (f32[1,1,1,8,128]{4,3,2,1,0:T(8,128)S(1)}, f32[1,1,1,8,128]{4,3,2,1,0:T(8,128)S(1)}, u32[]{:S(2)}, u32[]{:S(2)}) collective-permute-start(f32[1,1,1,8,128]{4,3,2,1,0:T(8,128)S(1)} %get-tuple-element.24), channel_id=1, source_target_pairs={{1,0},{2,1},{3,2},{0,3},{5,4},{6,5},{7,6},{4,7},{9,8},{10,9},{11,1... | collective-permute-start | bytes 12296 | tf_op jit(solution)/shard_map/ppermute | solution.py:15
  516.6 6.4 collective-permute-start.60
  516.6 8.1 %collective-permute-start.61 = (f32[1,1,1,8,128]{4,3,2,1,0:T(8,128)S(1)}, f32[1,1,1,8,128]{4,3,2,1,0:T(8,128)S(1)}, u32[]{:S(2)}, u32[]{:S(2)}) collective-permute-start(f32[1,1,1,8,128]{4,3,2,1,0:T(8,128)S(1)} %get-tuple-element.70), channel_id=1, source_target_pairs={{16,0},{0,16},{17,1},{1,17},{18,2},{2,18},{19,3},{3,19},{20,4},{4,... | collective-permute-start | bytes 12296 | tf_op jit(solution)/shard_map/ppermute | solution.py:15
  517.1 7.6 collective-permute-start.62
  536.8 7.3 collective-permute-start.67
  537.3 6.8 collective-permute-start.68
  537.9 6.1 collective-permute-start.69
  540.2 5.4 collective-permute-start.70
  585.1 6.0 collective-permute-start.72
  585.1 7.5 collective-permute-start.73
  585.6 7.1 collective-permute-start.74
  662.3 5.5 collective-permute-start.78
  664.9 6.8 collective-permute-start.79
  664.9 6.8 collective-permute-start.80
  666.4 9.4 %collective-permute-start.81 = (f32[1,1,1,8,128]{4,3,2,1,0:T(8,128)S(1)}, f32[1,1,1,8,128]{4,3,2,1,0:T(8,128)S(1)}, u32[]{:S(2)}, u32[]{:S(2)}) collective-permute-start(f32[1,1,1,8,128]{4,3,2,1,0:T(8,128)S(1)} %get-tuple-element.14), channel_id=1, source_target_pairs={{4,0},{8,4},{12,8},{0,12},{5,1},{9,5},{13,9},{1,13},{6,2},{10,6},{... | collective-permute-start | bytes 12296 | tf_op jit(solution)/shard_map/ppermute | solution.py:15
  667.9 8.0 %collective-permute-start.82 = (f32[1,1,1,8,128]{4,3,2,1,0:T(8,128)S(1)}, f32[1,1,1,8,128]{4,3,2,1,0:T(8,128)S(1)}, u32[]{:S(2)}, u32[]{:S(2)}) collective-permute-start(f32[1,1,1,8,128]{4,3,2,1,0:T(8,128)S(1)} %get-tuple-element.13), channel_id=1, source_target_pairs={{3,0},{0,1},{1,2},{2,3},{7,4},{4,5},{5,6},{6,7},{11,8},{8,9},{9,10... | collective-permute-start | bytes 12296 | tf_op jit(solution)/shard_map/ppermute | solution.py:15
  667.9 8.0 %collective-permute-start.83 = (f32[1,1,1,8,128]{4,3,2,1,0:T(8,128)S(1)}, f32[1,1,1,8,128]{4,3,2,1,0:T(8,128)S(1)}, u32[]{:S(2)}, u32[]{:S(2)}) collective-permute-start(f32[1,1,1,8,128]{4,3,2,1,0:T(8,128)S(1)} %get-tuple-element.12), channel_id=1, source_target_pairs={{1,0},{2,1},{3,2},{0,3},{5,4},{6,5},{7,6},{4,7},{9,8},{10,9},{11,1... | collective-permute-start | bytes 12296 | tf_op jit(solution)/shard_map/ppermute | solution.py:15
  718.4 6.4 collective-permute-start.84
  718.5 8.1 %collective-permute-start.85 = (f32[1,1,1,8,128]{4,3,2,1,0:T(8,128)S(1)}, f32[1,1,1,8,128]{4,3,2,1,0:T(8,128)S(1)}, u32[]{:S(2)}, u32[]{:S(2)}) collective-permute-start(f32[1,1,1,8,128]{4,3,2,1,0:T(8,128)S(1)} %get-tuple-element.58), channel_id=1, source_target_pairs={{16,0},{0,16},{17,1},{1,17},{18,2},{2,18},{19,3},{3,19},{20,4},{4,... | collective-permute-start | bytes 12296 | tf_op jit(solution)/shard_map/ppermute | solution.py:15
  719.0 7.6 collective-permute-start.86
  738.7 7.3 collective-permute-start.91
  739.2 6.8 collective-permute-start.92
  739.9 6.1 collective-permute-start.93
  (36 other events, 556.3 us)
where the time goes:
time: 789 us; the launch traced here: 788 us
  blocking collectives  555 us (70%)
  starting transfers between devices  131 us (17%)
  matrix products  43.7 us (6%)
  waiting for transfers between devices  36.2 us (5%)
  local copies, waits for them, and re-layouts  12.5 us (2%)
    all_gather x4, blocking collectives, coarse_weights(): lax.all_gather(on_modes, ('gx', 'gy', 'gz'), axis=0, tiled=True)  268 us
    psum x4, blocking collectives, energy_sum(): lax.psum(partial_inner(first, second), ('gx', 'gy', 'gz')).reshape(-1, 1, 1)  169 us
    ppermute x96, starting transfers between devices, from_behind(): return lax.ppermute(block, axis, route)  131 us
    psum x3, blocking collectives, on_device(): lax.psum(partial_inner(direction, dual_image), ('gx', 'gy', 'gz'))  118 us
    dot_general x4, matrix products, on_device(): jnp.dot(local_flattened, matrix, precision=highest)  40.3 us
    ppermute x96, waiting for transfers between devices, from_behind(): return lax.ppermute(block, axis, route)  36.2 us
  transfers between devices with their start and end apart: 96, of which 24 were waited for; matrix products, arithmetic and copies ran while one was open for 1% of the time, Pallas kernels for 0%

commit v1 on v0

v1 whole, which is shorter than its diff:
```python
import functools
import math

import jax
import jax.numpy as jnp
from jax import lax
from jax.experimental import pallas as pl
from jax.experimental.pallas import tpu as pltpu
from jax.sharding import PartitionSpec as P

ITERS = 4
NAMES = ("gx", "gy", "gz")
highest = lax.Precision.HIGHEST
SCALARS = 56


def dot_nt(a, b):
    return lax.dot_general(
        a, b, (((1,), (1,)), ((), ())), precision=highest, preferred_element_type=jnp.float32
    )


def dot_nn(a, b):
    return lax.dot_general(
        a, b, (((1,), (0,)), ((), ())), precision=highest, preferred_element_type=jnp.float32
    )


def kernel(
    sizes,
    k_hbm,
    modes,
    crows,
    loads,
    counts,
    contact,
    lam_out,
    res_out,
    kbuf,
    khi,
    klo,
    bmat,
    c7,
    act,
    rvec,
    yvec,
    faces_in,
    gath,
    k_sem,
    set_send,
    set_recv,
    face_send,
    face_recv,
    gath_send,
    gath_recv,
):
    cases = loads.shape[0]
    half = loads.shape[2]
    full = 2 * half
    local = bmat.shape[1]
    rigid = modes.shape[0]
    n = math.prod(sizes)
    pos = [lax.axis_index(name) for name in NAMES]
    me = (pos[0] * sizes[1] + pos[1]) * sizes[2] + pos[2]

    def neighbour(f):
        a = f // 2
        step = 1 if f % 2 else sizes[a] - 1
        where = list(pos)
        where[a] = lax.rem(pos[a] + step, sizes[a])
        return tuple(where)

    nbrs = [neighbour(f) for f in range(6)]

    def own_tile(f):
        return 2 * f + (1 - f % 2)

    def tile(f_tile):
        return slice(f_tile * half, (f_tile + 1) * half)

    def k_copy(c):
        return pltpu.make_async_copy(
            k_hbm.at[:, pl.ds(c * full, full)], kbuf.at[c], k_sem.at[c]
        )

    for c in range(6):
        k_copy(c).start()

    bmat[...] = jnp.zeros_like(bmat)
    c7[...] = jnp.zeros_like(c7)
    bmat[0:rigid, :] = modes[...]
    c7[0:rigid, 0 : crows.shape[1]] = crows[...]

    lane = lax.broadcasted_iota(jnp.int32, (cases, half), 1)
    for f in range(6):
        a = f // 2
        where = list(pos) if f % 2 else list(nbrs[f])
        count = counts[where[0], where[1], where[2], a]
        mask = (lane < count).astype(jnp.float32)
        act[:, tile(2 * f)] = mask
        act[:, tile(2 * f + 1)] = mask
        rvec[:, tile(own_tile(f))] = loads[:, f, :] * mask

    barrier = pltpu.get_barrier_semaphore()

    def greet(k, carry):
        pl.semaphore_signal(
            barrier,
            inc=1,
            device_id=lax.rem(me + k, n),
            device_id_type=pl.DeviceIdType.LOGICAL,
        )
        return carry

    lax.fori_loop(1, n, greet, 0)
    pl.semaphore_wait(barrier, n - 1)

    def remote(src, dst, send, recv, f):
        return pltpu.make_async_remote_copy(
            src_ref=src,
            dst_ref=dst,
            send_sem=send,
            recv_sem=recv,
            device_id=nbrs[f],
            device_id_type=pl.DeviceIdType.MESH,
        )

    def set_copies(f):
        opp = f ^ 1
        h = 1 - f % 2
        rows = pl.ds(8 * (opp + 1), 8)
        return [
            remote(
                rvec.at[:, pl.ds((2 * f + h) * half, half)],
                rvec.at[:, pl.ds((2 * opp + h) * half, half)],
                set_send.at[f, 0],
                set_recv.at[opp, 0],
                f,
            ),
            remote(
                bmat.at[pl.ds(0, 8), pl.ds(f * full, full)],
                bmat.at[rows, pl.ds(opp * full, full)],
                set_send.at[f, 1],
                set_recv.at[opp, 1],
                f,
            ),
            remote(c7.at[pl.ds(0, 8)], c7.at[rows], set_send.at[f, 2], set_recv.at[opp, 2], f),
        ]

    set_all = [set_copies(f) for f in range(6)]
    for i in range(3):
        for f in range(6):
            set_all[f][i].start()

    def split_chunk(c):
        k_copy(c).wait()
        step = 256

        def body(i, carry):
            rows = pl.ds(pl.multiple_of(i * step, step), step)
            x = kbuf[c, rows, :]
            hi = x.astype(jnp.bfloat16)
            khi[c, rows, :] = hi
            klo[c, rows, :] = (x - hi.astype(jnp.float32)).astype(jnp.bfloat16)
            return carry

        lax.fori_loop(0, local // step, body, 0)

    def send_message(p, message):
        rolled = pltpu.roll(message, half // 2, 1)
        packed = jnp.where(
            lane[0 : cases // 2] < half // 2, message[0 : cases // 2], rolled[cases // 2 :]
        )
        gath[p, me] = packed

        def body(k, carry):
            pltpu.make_async_remote_copy(
                src_ref=gath.at[p, me],
                dst_ref=gath.at[p, me],
                send_sem=gath_send.at[p],
                recv_sem=gath_recv.at[p],
                device_id=lax.rem(me + k, n),
                device_id_type=pl.DeviceIdType.LOGICAL,
            ).start()
            return carry

        lax.fori_loop(1, n, body, 0)

    def gather_bytes(p):
        block = gath.at[p, pl.ds(0, n - 1)]
        return pltpu.make_async_remote_copy(
            src_ref=block,
            dst_ref=block,
            send_sem=gath_send.at[p],
            recv_sem=gath_recv.at[p],
            device_id=lax.rem(me + 1, n),
            device_id_type=pl.DeviceIdType.LOGICAL,
        )

    def received(p):
        packed = gath[p]
        other = pltpu.roll(packed.reshape(n * cases // 2, half), half // 2, 1).reshape(
            packed.shape
        )
        return jnp.concatenate([packed, other], axis=1)

    tiles_e = c7.shape[1] // half

    def coarse_sum(blocks, only_own):
        terms = blocks
        if not only_own:
            flat = blocks.reshape(n * cases, half)
            for f in range(6):
                moved = pltpu.roll(flat, half - 8 * (f + 1), 1).reshape(
                    sizes + (cases, half)
                )
                moved = jnp.roll(moved, 1 if f % 2 else -1, axis=f // 2)
                terms = terms + moved.reshape(n, cases, half)
        sums = [jnp.zeros((cases, half), jnp.float32) for _ in range(tiles_e)]
        for s in range(n):
            low = rigid * s
            moved = pltpu.roll(terms[s], low % half, 1) if low % half else terms[s]
            for q in range(low // half, (low + rigid - 1) // half + 1):
                at = lane + half * q
                sums[q] = jnp.where((at >= low) & (at < low + rigid), moved, sums[q])
        return jnp.concatenate(sums, axis=1)

    def own_inner(first, second):
        total = jnp.zeros((cases, half), jnp.float32)
        for f in range(6):
            cut = tile(own_tile(f))
            total = total + first[:, cut] * second[:, cut]
        return jnp.sum(total, axis=1, keepdims=True)

    def all_inner(first, second):
        total = jnp.zeros((cases, half), jnp.float32)
        for t in range(12):
            total = total + first[:, tile(t)] * second[:, tile(t)]
        return jnp.sum(total, axis=1, keepdims=True)

    split_chunk(0)
    split_chunk(1)
    for f in range(6):
        for i in range(2):
            set_all[f][i].wait_recv()
    residual = rvec[...]
    first_terms = dot_nt(residual, bmat[0:8, :])
    send_message(
        0, jnp.concatenate([first_terms, jnp.zeros((cases, half - 8), jnp.float32)], axis=1)
    )
    for c in range(2, 6):
        split_chunk(c)
    for f in range(6):
        set_all[f][2].wait_recv()
        for i in range(3):
            set_all[f][i].wait_send()
    gather_bytes(0).wait_recv()
    alpha = dot_nt(coarse_sum(received(0), True), c7[...])
    active = act[...]
    z = residual - active * dot_nn(alpha, bmat[...])

    face_copies = []
    lam = [jnp.zeros((cases, half), jnp.float32) for _ in range(6)]
    direction = image = alpha_image = energy = curvature = None
    for it in range(ITERS):
        last = it + 1 == ITERS
        p = it + 1
        hi = z.astype(jnp.bfloat16)
        lo = (z - hi.astype(jnp.float32)).astype(jnp.bfloat16)
        parts = jnp.concatenate([hi, lo], axis=0)
        copies = []
        ys = []
        for f in range(6):
            yf = jnp.dot(parts, khi[f], preferred_element_type=jnp.float32) + jnp.dot(
                parts, klo[f], preferred_element_type=jnp.float32
            )
            yf = yf[0:cases] + yf[cases:]
            yvec[it, f] = yf
            copy = remote(
                yvec.at[it, f], faces_in.at[it, f ^ 1], face_send.at[it, f],
                face_recv.at[it, f ^ 1], f,
            )
            copy.start()
            copies.append(copy)
            ys.append(yf)
        y = jnp.concatenate(ys, axis=1)
        scalars = [all_inner(z, y), own_inner(rvec, z)]
        if it:
            scalars.append(own_inner(z, image))
        if last:
            message = jnp.zeros((cases, half), jnp.float32)
        else:
            terms = dot_nt(y * active, bmat[...])
            message = jnp.concatenate([terms, jnp.zeros_like(terms)], axis=1)
        for i, value in enumerate(scalars):
            message = jnp.where(lane == SCALARS + i, value, message)
        send_message(p, message)

        for f in range(6):
            copies[f].wait_recv()
        y = jnp.concatenate([ys[f] + faces_in[it, f] for f in range(6)], axis=1) * active
        gather_bytes(p).wait_recv()
        blocks = received(p)
        totals = jnp.sum(blocks, axis=0)
        along = totals[:, SCALARS : SCALARS + 1]
        energy_next = totals[:, SCALARS + 1 : SCALARS + 2]
        if it == 0:
            direction, image, curvature = z, y, along
        else:
            ratio = energy_next / energy
            across = totals[:, SCALARS + 2 : SCALARS + 3]
            direction = z + ratio * direction
            image = y + ratio * image
            curvature = along + 2.0 * ratio * across + ratio * ratio * curvature
        energy = energy_next
        step_size = energy / curvature
        rvec[...] = rvec[...] - step_size * image
        if not last:
            alpha_y = dot_nt(coarse_sum(blocks, False), c7[...])
            alpha_image = alpha_y if it == 0 else alpha_y + ratio * alpha_image
            alpha = alpha - step_size * alpha_image
            z = rvec[...] - active * dot_nn(alpha, bmat[...])
        for f in range(6):
            updated = lam[f] + step_size * direction[:, tile(own_tile(f))]
            lam[f] = jnp.where(contact[f : f + 1, :] == 1, jnp.maximum(updated, 0.0), updated)
        face_copies.extend(copies)

    for f in range(6):
        lam_out[:, f, :] = lam[f]
        res_out[:, f, :] = rvec[:, tile(own_tile(f))]
    for copy in face_copies:
        copy.wait_send()
    for p in range(ITERS + 1):
        gather_bytes(p).wait_send()


def on_device(sizes, dual_matrix, modes, coarse_rows, loads, face_counts, contact):
    cases, faces, half = loads.shape[3:]
    local = dual_matrix.shape[-1]
    rigid = modes.shape[-2]
    full = 2 * half
    n = math.prod(sizes)
    width = -(-coarse_rows.shape[1] // half) * half
    vmem = pl.BlockSpec(memory_space=pltpu.VMEM)
    dma = pltpu.SemaphoreType.DMA
    f32 = jnp.float32
    out = jax.ShapeDtypeStruct((cases, faces, half), f32)
    lam, res = pl.pallas_call(
        functools.partial(kernel, sizes),
        out_shape=(out, out),
        in_specs=[
            pl.BlockSpec(memory_space=pl.ANY),
            vmem,
            vmem,
            vmem,
            pl.BlockSpec(memory_space=pltpu.SMEM),
            vmem,
        ],
        out_specs=(vmem, vmem),
        scratch_shapes=[
            pltpu.VMEM((faces, local, full), f32),
            pltpu.VMEM((faces, local, full), jnp.bfloat16),
            pltpu.VMEM((faces, local, full), jnp.bfloat16),
            pltpu.VMEM((64, local), f32),
            pltpu.VMEM((64, width), f32),
            pltpu.VMEM((cases, local), f32),
            pltpu.VMEM((cases, local), f32),
            pltpu.VMEM((ITERS, faces, cases, full), f32),
            pltpu.VMEM((ITERS, faces, cases, full), f32),
            pltpu.VMEM((ITERS + 1, n, cases // 2, half), f32),
            dma((faces,)),
            dma((faces, 3)),
            dma((faces, 3)),
            dma((ITERS, faces)),
            dma((ITERS, faces)),
            dma((ITERS + 1,)),
            dma((ITERS + 1,)),
        ],
        compiler_params=pltpu.CompilerParams(
            collective_id=0, has_side_effects=True, vmem_limit_bytes=48 * 1024 * 1024
        ),
    )(
        dual_matrix.reshape(local, local),
        modes.reshape(rigid, local),
        coarse_rows,
        loads.reshape(cases, faces, half),
        face_counts,
        contact.reshape(faces, half),
    )
    return lam.reshape(loads.shape), res.reshape(loads.shape)


def solution(mesh):
    sizes = tuple(mesh.shape[name] for name in NAMES)
    return jax.shard_map(
        functools.partial(on_device, sizes),
        mesh=mesh,
        in_specs=(
            P("gx", "gy", "gz", None, None),
            P("gx", "gy", "gz", None, None),
            P(("gx", "gy", "gz"), None),
            P("gx", "gy", "gz", None, None, None),
            P(),
            P("gx", "gy", "gz", None, None),
        ),
        out_specs=(P("gx", "gy", "gz", None, None, None), P("gx", "gy", "gz", None, None, None)),
        check_vma=False,
    )
```

time: 789 us -> 60.1 us (0.08)
  blocking collectives: 555 us -> 0 us
  starting transfers between devices: 131 us -> 0 us
  Pallas kernels: 0 us -> 54.1 us
  matrix products: 43.7 us -> 0 us
  waiting for transfers between devices: 36.2 us -> 0 us
    psum x7 -> x0, blocking collectives: 287 us -> none  [the longest x4 169 us: energy_sum(): lax.psum(partial_inner(first, second), ('gx', 'gy', 'gz')).reshape(-1, 1, 1)]
    all_gather x4 -> x0, blocking collectives: 268 us -> none  [coarse_weights(): lax.all_gather(on_modes, ('gx', 'gy', 'gz'), axis=0, tiled=True)]
    ppermute x96 -> x0, starting transfers between devices: 131 us -> none  [from_behind(): return lax.ppermute(block, axis, route)]
    pallas_call x0 -> x1, Pallas kernels: none -> 54.1 us  [on_device(): pl.pallas_call(functools.partial(kernel, sizes), out_shape=(out, out), in...]
    dot_general x16 -> x0, matrix products: 43.7 us -> none  [the longest x4 40.3 us: on_device(): jnp.dot(local_flattened, matrix, precision=highest)]
    ppermute x96 -> x0, waiting for transfers between devices: 36.2 us -> none  [from_behind(): return lax.ppermute(block, axis, route)]
  transfers between devices with their start and end apart: 96 -> 0, of which waited for: 24 -> 0; matrix products, arithmetic and copies ran while one was open for 1% -> 0% of each run, Pallas kernels for 0% -> 0%
where the time goes in v1:
time: 60.1 us; the launch traced here: 59.7 us
  Pallas kernels  54.1 us (90%)
  local copies, waits for them, and re-layouts  4.96 us (8%)
  between operations  0.64 us (1%)
    pallas_call x1, Pallas kernels, on_device(): pl.pallas_call(functools.partial(kernel, sizes), out_shape=(out, out), in...  54.1 us
    unnamed x8, local copies, waits for them, and re-layouts  4.96 us

profile of v1, /device:TPU:0, one launch (start us, length us, event | category | flops | bytes accessed | tf_op | source)
XLA Modules:
  0.0 59.7 jit_solution(1741221011682186100)
XLA Ops:
  0.6 0.7 %copy.19 = s32[1,1,1,6,128]{4,3,2,1,0:T(8,128)S(1)} copy(s32[1,1,1,6,128]{4,2,3,1,0:T(1,128)} %param.11) | data formatting | bytes 6144
  1.3 0.8 %copy.9.counts = s32[2,4,4,3]{3,2,1,0:T(4,128)S(1)} copy(s32[2,4,4,3]{2,1,3,0:T(4,128)} %param.10) | data formatting | bytes 768 | tf_op args[4]
  2.2 0.7 %copy.18 = f32[1,1,1,8,6,128]{5,4,3,2,1,0:T(8,128)S(1)} copy(f32[1,1,1,8,6,128]{5,3,4,2,1,0:T(8,128)} %param.9) | data formatting | bytes 49152 | tf_op args[3]
  2.9 0.8 %copy.17 = f32[1,1,1,6,1536]{4,3,2,1,0:T(8,128)S(1)} copy(f32[1,1,1,6,1536]{4,2,3,1,0:T(1,128)} %param.7) | data formatting | bytes 73728
  3.7 0.0 copy-start
  3.7 0.7 %copy-done = f32[6,192]{1,0:T(8,128)S(1)} copy-done((f32[6,192]{1,0:T(8,128)S(1)}, f32[6,192]{1,0:T(8,128)}, u32[]{:S(2)}) %copy-start) | copy-done | bytes 4632
  4.4 54.1 %shard_map.77 = (f32[8,6,128]{2,1,0:T(8,128)S(1)}, f32[8,6,128]{2,1,0:T(8,128)S(1)}) custom-call(f32[1536,1536]{1,0:T(8,128)} %bitcast.17, f32[6,1536]{1,0:T(8,128)S(1)} %bitcast.12, f32[6,192]{1,0:T(8,128)S(1)} %copy-done, f32[8,6,128]{2,1,0:T(8,128)S(1)} %bitcast.13, s32[2,4,4,3]{3,2,1,0:T(4,128)S(1)} %copy.9.counts, s32[6,128]{1,0:T(8,128)S(1)} %bitcast.16), custom_call_target="tpu_custom_call" | custom-call | tf_op jit(solution)/shard_map/pallas_call | solution.py:348
  58.5 0.6 %copy.10 = f32[1,1,1,8,6,128]{5,3,4,2,1,0:T(8,128)} copy(f32[1,1,1,8,6,128]{5,4,3,2,1,0:T(8,128)S(1)} %bitcast.15) | data formatting | bytes 49152
  59.1 0.6 %copy.11 = f32[1,1,1,8,6,128]{5,3,4,2,1,0:T(8,128)} copy(f32[1,1,1,8,6,128]{5,4,3,2,1,0:T(8,128)S(1)} %bitcast.14) | data formatting | bytes 49152
Async XLA Ops:
  3.7 0.7 %copy-start = (f32[6,192]{1,0:T(8,128)S(1)}, f32[6,192]{1,0:T(8,128)}, u32[]{:S(2)}) copy-start(f32[6,192]{1,0:T(8,128)} %crows.1) | copy-start | bytes 13828

commit v2 on v1

--- a/solution.py
+++ b/solution.py
@@ -10,30 +10,38 @@
 
 ITERS = 4
 NAMES = ("gx", "gy", "gz")
-highest = lax.Precision.HIGHEST
 SCALARS = 56
 
 
-def dot_nt(a, b):
-    return lax.dot_general(
-        a, b, (((1,), (1,)), ((), ())), precision=highest, preferred_element_type=jnp.float32
-    )
-
-
-def dot_nn(a, b):
-    return lax.dot_general(
-        a, b, (((1,), (0,)), ((), ())), precision=highest, preferred_element_type=jnp.float32
-    )
+def split(x):
+    hi = x.astype(jnp.bfloat16)
+    return hi, (x - hi.astype(jnp.float32)).astype(jnp.bfloat16)
+
+
+def split_dot(parts, hi, lo, contract):
+    dims = (((1,), (contract,)), ((), ()))
+    both = lax.dot_general(parts, hi, dims, preferred_element_type=jnp.float32)
+    both = both + lax.dot_general(parts, lo, dims, preferred_element_type=jnp.float32)
+    rows = parts.shape[0] // 2
+    return both[0:rows] + both[rows:]
+
+
+def dot_nt(a, hi, lo):
+    return split_dot(jnp.concatenate(split(a), axis=0), hi, lo, 1)
+
+
+def dot_nn(a, hi, lo):
+    return split_dot(jnp.concatenate(split(a), axis=0), hi, lo, 0)
 
 
 def kernel(
     sizes,
     k_hbm,
-    modes,
-    crows,
-    loads,
+    modes_in,
+    crows_in,
+    loads_in,
     counts,
-    contact,
+    contact_in,
     lam_out,
     res_out,
     kbuf,
@@ -46,7 +54,16 @@
     yvec,
     faces_in,
     gath,
+    modes,
+    crows,
+    loads,
+    contact,
+    bhi,
+    blo,
+    chi,
+    clo,
     k_sem,
+    in_sem,
     set_send,
     set_recv,
     face_send,
@@ -54,11 +71,11 @@
     gath_send,
     gath_recv,
 ):
-    cases = loads.shape[0]
+    cases = loads.shape[1]
     half = loads.shape[2]
     full = 2 * half
     local = bmat.shape[1]
-    rigid = modes.shape[0]
+    rigid = modes_in.shape[0]
     n = math.prod(sizes)
     pos = [lax.axis_index(name) for name in NAMES]
     me = (pos[0] * sizes[1] + pos[1]) * sizes[2] + pos[2]
@@ -83,24 +100,19 @@
             k_hbm.at[:, pl.ds(c * full, full)], kbuf.at[c], k_sem.at[c]
         )
 
+    small = [
+        pltpu.make_async_copy(src, dst, in_sem.at[i])
+        for i, (src, dst) in enumerate(
+            ((loads_in, loads), (modes_in, modes), (crows_in, crows), (contact_in, contact))
+        )
+    ]
+    for copy in small:
+        copy.start()
     for c in range(6):
         k_copy(c).start()
 
     bmat[...] = jnp.zeros_like(bmat)
     c7[...] = jnp.zeros_like(c7)
-    bmat[0:rigid, :] = modes[...]
-    c7[0:rigid, 0 : crows.shape[1]] = crows[...]
-
-    lane = lax.broadcasted_iota(jnp.int32, (cases, half), 1)
-    for f in range(6):
-        a = f // 2
-        where = list(pos) if f % 2 else list(nbrs[f])
-        count = counts[where[0], where[1], where[2], a]
-        mask = (lane < count).astype(jnp.float32)
-        act[:, tile(2 * f)] = mask
-        act[:, tile(2 * f + 1)] = mask
-        rvec[:, tile(own_tile(f))] = loads[:, f, :] * mask
-
     barrier = pltpu.get_barrier_semaphore()
 
     def greet(k, carry):
@@ -113,6 +125,22 @@
         return carry
 
     lax.fori_loop(1, n, greet, 0)
+    for copy in small:
+        copy.wait()
+    for m in range(rigid):
+        bmat[m : m + 1, :] = modes[m]
+    c7[0:rigid, 0 : crows.shape[1]] = crows[...]
+
+    lane = lax.broadcasted_iota(jnp.int32, (cases, half), 1)
+    for f in range(6):
+        a = f // 2
+        where = list(pos) if f % 2 else list(nbrs[f])
+        count = counts[where[0], a, where[1], where[2]]
+        mask = (lane < count).astype(jnp.float32)
+        act[:, tile(2 * f)] = mask
+        act[:, tile(2 * f + 1)] = mask
+        rvec[:, tile(own_tile(f))] = loads[f] * mask
+
     pl.semaphore_wait(barrier, n - 1)
 
     def remote(src, dst, send, recv, f):
@@ -159,9 +187,7 @@
         def body(i, carry):
             rows = pl.ds(pl.multiple_of(i * step, step), step)
             x = kbuf[c, rows, :]
-            hi = x.astype(jnp.bfloat16)
-            khi[c, rows, :] = hi
-            klo[c, rows, :] = (x - hi.astype(jnp.float32)).astype(jnp.bfloat16)
+            khi[c, rows, :], klo[c, rows, :] = split(x)
             return carry
 
         lax.fori_loop(0, local // step, body, 0)
@@ -244,20 +270,22 @@
         for i in range(2):
             set_all[f][i].wait_recv()
     residual = rvec[...]
-    first_terms = dot_nt(residual, bmat[0:8, :])
+    first_terms = dot_nt(residual, *split(bmat[0:8, :]))
     send_message(
         0, jnp.concatenate([first_terms, jnp.zeros((cases, half - 8), jnp.float32)], axis=1)
     )
+    bhi[...], blo[...] = split(bmat[...])
     for c in range(2, 6):
         split_chunk(c)
     for f in range(6):
         set_all[f][2].wait_recv()
         for i in range(3):
             set_all[f][i].wait_send()
+    chi[...], clo[...] = split(c7[...])
     gather_bytes(0).wait_recv()
-    alpha = dot_nt(coarse_sum(received(0), True), c7[...])
+    alpha = dot_nt(coarse_sum(received(0), True), chi[...], clo[...])
     active = act[...]
-    z = residual - active * dot_nn(alpha, bmat[...])
+    z = residual - active * dot_nn(alpha, bhi[...], blo[...])
 
     face_copies = []
     lam = [jnp.zeros((cases, half), jnp.float32) for _ in range(6)]
@@ -265,24 +293,19 @@
     for it in range(ITERS):
         last = it + 1 == ITERS
         p = it + 1
-        hi = z.astype(jnp.bfloat16)
-        lo = (z - hi.astype(jnp.float32)).astype(jnp.bfloat16)
-        parts = jnp.concatenate([hi, lo], axis=0)
-        copies = []
-        ys = []
-        for f in range(6):
-            yf = jnp.dot(parts, khi[f], preferred_element_type=jnp.float32) + jnp.dot(
-                parts, klo[f], preferred_element_type=jnp.float32
-            )
-            yf = yf[0:cases] + yf[cases:]
+        parts = jnp.concatenate(split(z), axis=0)
+        copies = [None] * 6
+        ys = [None] * 6
+        for f in (4, 5, 2, 3, 0, 1):
+            yf = split_dot(parts, khi[f], klo[f], 0)
             yvec[it, f] = yf
             copy = remote(
                 yvec.at[it, f], faces_in.at[it, f ^ 1], face_send.at[it, f],
                 face_recv.at[it, f ^ 1], f,
             )
             copy.start()
-            copies.append(copy)
-            ys.append(yf)
+            copies[f] = copy
+            ys[f] = yf
         y = jnp.concatenate(ys, axis=1)
         scalars = [all_inner(z, y), own_inner(rvec, z)]
         if it:
@@ -290,7 +313,7 @@
         if last:
             message = jnp.zeros((cases, half), jnp.float32)
         else:
-            terms = dot_nt(y * active, bmat[...])
+            terms = dot_nt(y * active, bhi[...], blo[...])
             message = jnp.concatenate([terms, jnp.zeros_like(terms)], axis=1)
         for i, value in enumerate(scalars):
             message = jnp.where(lane == SCALARS + i, value, message)
@@ -316,18 +339,18 @@
         step_size = energy / curvature
         rvec[...] = rvec[...] - step_size * image
         if not last:
-            alpha_y = dot_nt(coarse_sum(blocks, False), c7[...])
+            alpha_y = dot_nt(coarse_sum(blocks, False), chi[...], clo[...])
             alpha_image = alpha_y if it == 0 else alpha_y + ratio * alpha_image
             alpha = alpha - step_size * alpha_image
-            z = rvec[...] - active * dot_nn(alpha, bmat[...])
+            z = rvec[...] - active * dot_nn(alpha, bhi[...], blo[...])
         for f in range(6):
             updated = lam[f] + step_size * direction[:, tile(own_tile(f))]
-            lam[f] = jnp.where(contact[f : f + 1, :] == 1, jnp.maximum(updated, 0.0), updated)
+            lam[f] = jnp.where(contact[f] == 1, jnp.maximum(updated, 0.0), updated)
         face_copies.extend(copies)
 
     for f in range(6):
-        lam_out[:, f, :] = lam[f]
-        res_out[:, f, :] = rvec[:, tile(own_tile(f))]
+        lam_out[f] = lam[f]
+        res_out[f] = rvec[:, tile(own_tile(f))]
     for copy in face_copies:
         copy.wait_send()
     for p in range(ITERS + 1):
@@ -341,20 +364,21 @@
     full = 2 * half
     n = math.prod(sizes)
     width = -(-coarse_rows.shape[1] // half) * half
+    hbm = pl.BlockSpec(memory_space=pl.ANY)
     vmem = pl.BlockSpec(memory_space=pltpu.VMEM)
     dma = pltpu.SemaphoreType.DMA
     f32 = jnp.float32
-    out = jax.ShapeDtypeStruct((cases, faces, half), f32)
+    out = jax.ShapeDtypeStruct((faces, cases, half), f32)
     lam, res = pl.pallas_call(
         functools.partial(kernel, sizes),
         out_shape=(out, out),
         in_specs=[
-            pl.BlockSpec(memory_space=pl.ANY),
-            vmem,
-            vmem,
-            vmem,
+            hbm,
+            hbm,
+            hbm,
+            hbm,
             pl.BlockSpec(memory_space=pltpu.SMEM),
-            vmem,
+            hbm,
         ],
         out_specs=(vmem, vmem),
         scratch_shapes=[
@@ -368,7 +392,16 @@
             pltpu.VMEM((ITERS, faces, cases, full), f32),
             pltpu.VMEM((ITERS, faces, cases, full), f32),
             pltpu.VMEM((ITERS + 1, n, cases // 2, half), f32),
+            pltpu.VMEM((rigid, 1, local), f32),
+            pltpu.VMEM(coarse_rows.shape, f32),
+            pltpu.VMEM((faces, cases, half), f32),
+            pltpu.VMEM((faces, 1, half), jnp.int32),
+            pltpu.VMEM((64, local), jnp.bfloat16),
+            pltpu.VMEM((64, local), jnp.bfloat16),
+            pltpu.VMEM((64, width), jnp.bfloat16),
+            pltpu.VMEM((64, width), jnp.bfloat16),
             dma((faces,)),
+            dma((4,)),
             dma((faces, 3)),
             dma((faces, 3)),
             dma((ITERS, faces)),
@@ -377,17 +410,20 @@
             dma((ITERS + 1,)),
         ],
         compiler_params=pltpu.CompilerParams(
-            collective_id=0, has_side_effects=True, vmem_limit_bytes=48 * 1024 * 1024
+            collective_id=0, has_side_effects=True, vmem_limit_bytes=64 * 1024 * 1024
         ),
     )(
         dual_matrix.reshape(local, local),
-        modes.reshape(rigid, local),
+        modes.reshape(rigid, 1, local),
         coarse_rows,
-        loads.reshape(cases, faces, half),
-        face_counts,
-        contact.reshape(faces, half),
+        loads.reshape(cases, faces, half).transpose(1, 0, 2),
+        face_counts.transpose(0, 3, 1, 2),
+        contact.reshape(faces, 1, half),
     )
-    return lam.reshape(loads.shape), res.reshape(loads.shape)
+    return (
+        lam.transpose(1, 0, 2).reshape(loads.shape),
+        res.transpose(1, 0, 2).reshape(loads.shape),
+    )
 
 
 def solution(mesh):

time: 60.1 us -> 56.5 us (0.940)
  local copies, waits for them, and re-layouts: 4.96 us -> 2.69 us
  Pallas kernels: 54.1 us -> 52.9 us
    unnamed x8 -> x2, local copies, waits for them, and re-layouts: 4.96 us -> 2.69 us
    pallas_call x1, Pallas kernels: 54.1 us -> 52.9 us  [on_device(): pl.pallas_call(functools.partial(kernel, sizes), out_shape=(out, out), in...]
where the time goes in v2:
time: 56.5 us; the launch traced here: 56.2 us
  Pallas kernels  52.9 us (94%)
  local copies, waits for them, and re-layouts  2.69 us (5%)
  between operations  0.64 us (1%)
    pallas_call x1, Pallas kernels, on_device(): pl.pallas_call(functools.partial(kernel, sizes), out_shape=(out, out), in...  52.9 us
    unnamed x2, local copies, waits for them, and re-layouts  2.69 us

profile of v2, /device:TPU:0, one launch (start us, length us, event | category | flops | bytes accessed | tf_op | source)
XLA Modules:
  0.0 56.2 jit_solution(5236285970692119584)
XLA Ops:
  0.6 52.9 %shard_map.77 = (f32[6,8,128]{2,1,0:T(8,128)}, f32[6,8,128]{2,1,0:T(8,128)}) custom-call(f32[1536,1536]{1,0:T(8,128)} %bitcast.13, f32[6,1,1536]{2,1,0:T(1,128)} %bitcast.14, f32[6,192]{1,0:T(8,128)} %crows_in.1, f32[6,8,128]{2,1,0:T(8,128)} %bitcast.17, s32[2,3,4,4]{3,2,1,0:T(4,128)} %bitcast.18, s32[6,1,128]{2,1,0:T(1,128)} %bitcast.19), custom_call_target="tpu_custom_call" | custom-call | tf_op jit(solution)/shard_map/pallas_call | solution.py:372
  53.5 1.3 %copy.10 = f32[1,1,1,8,6,128]{5,3,4,2,1,0:T(8,128)} copy(f32[1,1,1,8,6,128]{5,3,4,2,1,0:T(8,128)} %bitcast.16) | data formatting | bytes 49152
  54.9 1.3 %copy.11 = f32[1,1,1,8,6,128]{5,3,4,2,1,0:T(8,128)} copy(f32[1,1,1,8,6,128]{5,3,4,2,1,0:T(8,128)} %bitcast.15) | data formatting | bytes 49152

commit v3 on v2

--- a/solution.py
+++ b/solution.py
@@ -303,7 +303,6 @@
                 yvec.at[it, f], faces_in.at[it, f ^ 1], face_send.at[it, f],
                 face_recv.at[it, f ^ 1], f,
             )
-            copy.start()
             copies[f] = copy
             ys[f] = yf
         y = jnp.concatenate(ys, axis=1)
@@ -318,6 +317,8 @@
         for i, value in enumerate(scalars):
             message = jnp.where(lane == SCALARS + i, value, message)
         send_message(p, message)
+        for f in (4, 5, 2, 3, 0, 1):
+            copies[f].start()
 
         for f in range(6):
             copies[f].wait_recv()

time: 56.5 us -> 49.8 us (0.88)
  Pallas kernels: 52.9 us -> 46.2 us
    pallas_call x1, Pallas kernels: 52.9 us -> 46.2 us  [on_device(): pl.pallas_call(functools.partial(kernel, sizes), out_shape=(out, out), in...]
where the time goes in v3:
time: 49.8 us; the launch traced here: 49.5 us
  Pallas kernels  46.2 us (93%)
  local copies, waits for them, and re-layouts  2.69 us (5%)
  between operations  0.64 us (1%)
    pallas_call x1, Pallas kernels, on_device(): pl.pallas_call(functools.partial(kernel, sizes), out_shape=(out, out), in...  46.2 us
    unnamed x2, local copies, waits for them, and re-layouts  2.69 us

profile of v3, /device:TPU:0, one launch (start us, length us, event | category | flops | bytes accessed | tf_op | source)
XLA Modules:
  0.0 49.5 jit_solution(3887745104689732769)
XLA Ops:
  0.6 46.2 %shard_map.77 = (f32[6,8,128]{2,1,0:T(8,128)}, f32[6,8,128]{2,1,0:T(8,128)}) custom-call(f32[1536,1536]{1,0:T(8,128)} %bitcast.13, f32[6,1,1536]{2,1,0:T(1,128)} %bitcast.14, f32[6,192]{1,0:T(8,128)} %crows_in.1, f32[6,8,128]{2,1,0:T(8,128)} %bitcast.17, s32[2,3,4,4]{3,2,1,0:T(4,128)} %bitcast.18, s32[6,1,128]{2,1,0:T(1,128)} %bitcast.19), custom_call_target="tpu_custom_call" | custom-call | tf_op jit(solution)/shard_map/pallas_call | solution.py:373
  46.8 1.3 %copy.10 = f32[1,1,1,8,6,128]{5,3,4,2,1,0:T(8,128)} copy(f32[1,1,1,8,6,128]{5,3,4,2,1,0:T(8,128)} %bitcast.16) | data formatting | bytes 49152
  48.1 1.3 %copy.11 = f32[1,1,1,8,6,128]{5,3,4,2,1,0:T(8,128)} copy(f32[1,1,1,8,6,128]{5,3,4,2,1,0:T(8,128)} %bitcast.15) | data formatting | bytes 49152
